TPU v7x, 512 devices: a whole 4x8x8 slice. The times are simulated.
512 devices in a mesh: seq: 128 (over z_lo, x, y, core), head: 4 (over z_hi).
Axes of the slice: x: 4, y: 8, z: 8 (z_hi: 4, z_lo: 2; z = z_hi * 2 + z_lo), core: 2. Of those that a mesh axis runs over, the one named last changes fastest.
Arguments:
- queries: bfloat16 [16384, 4096], P('seq', 'head'), may hold values from -6 to 6
- key_rows: bfloat16 [16384, 4096], P('seq', 'head'), may hold values from -6 to 6
- values: bfloat16 [16384, 4096], P('seq', 'head'), may hold values from -11 to 11
- out_grad: bfloat16 [16384, 4096], P('seq', 'head'), may hold values from -11 to 11
- norm_gain: float32 [4096], P('head'), may hold values from 0.1 to 1.9
- head_levels: int32 [32, 7], P('head'), may hold values 0 or 1
Outputs:
- normed: bfloat16 [16384, 4096], P('seq', 'head')
- query_grad: bfloat16 [16384, 4096], P('seq', 'head')
- key_grad: bfloat16 [16384, 4096], P('seq', 'head')
- value_grad: bfloat16 [16384, 4096], P('seq', 'head')
- gain_grad: float32 [4096], P('head')
Inputs may be any that keep to these rules, and one draw needn't show every extreme that they name: head_levels[h, l] is 1 where head h reads the block 2**l blocks back.
All inputs are finite; a program needn't handle non-finite values.
Results may differ from a plain program's by a relative error of at most 0.018.
Values may be sent and summed in bfloat16 or wider, within the bound.
A program may use at most 64 MiB of HBM per device.

v0:
```python
import math
import jax
import jax.numpy as jnp
from jax import lax
from jax.sharding import PartitionSpec as P

D = 4096
HEAD_DIM = 128
EPSILON = 1e-06


def shifted(x, axis, by):
    devices = lax.axis_size(axis)
    pairs = [(i, i + by) for i in range(devices) if 0 <= i + by < devices]
    return lax.ppermute(x, axis, pairs)


def column_block(matrix, which_head, head_size):
    return lax.dynamic_slice_in_dim(matrix, which_head * head_size, head_size, 1)


def place_cols(buffer, portion, which_head, head_size):
    return lax.dynamic_update_slice_in_dim(buffer, portion, which_head * head_size, 1)


def contract_cols(left_side, right_side):
    return lax.dot_general(
        left_side, right_side, (((1,), (1,)), ((), ())), preferred_element_type=jnp.float32
    )


def contract_rows(left_side, right_side):
    return lax.dot_general(
        left_side, right_side, (((0,), (0,)), ((), ())), preferred_element_type=jnp.float32
    )


def body(queries, key_rows, values, out_grad, norm_gain, head_levels):
    f32 = jnp.float32
    bf16 = jnp.bfloat16
    tok_rows, row_width = queries.shape
    head_size = HEAD_DIM
    local_heads = row_width // head_size
    seq_devices = lax.axis_size("seq")
    level_count = seq_devices.bit_length() - 1
    block_index = lax.axis_index("seq")
    score_scale = 1.0 / math.sqrt(head_size)
    fetched = []
    for exponent in range(level_count):
        fetched.append(shifted((key_rows, values), "seq", 2**exponent))
    near_keys = jnp.concatenate([key_rows] + [received[0] for received in fetched], axis=0)
    near_values = jnp.concatenate([values] + [received[1] for received in fetched], axis=0)
    key_count = near_keys.shape[0]
    distance = 2 ** jnp.arange(level_count, dtype=jnp.int32)
    level_live = (head_levels == 1) & (block_index >= distance)[None, :]
    block_live = jnp.concatenate([jnp.ones((local_heads, 1), jnp.bool_), level_live], axis=1)
    key_block = jnp.arange(key_count, dtype=jnp.int32) // tok_rows
    key_place = jnp.arange(key_count, dtype=jnp.int32) % tok_rows
    row_place = jnp.arange(tok_rows, dtype=jnp.int32)
    causal = (key_block[None, :] > 0) | (key_place[None, :] <= row_place[:, None])
    block_hit = key_block[None, :] == jnp.arange(level_count + 1, dtype=jnp.int32)[:, None]

    def forward_head(which_head, buffers):
        context, weight_store, max_store, sum_store = buffers
        query_head = column_block(queries, which_head, head_size)
        key_head = column_block(near_keys, which_head, head_size)
        value_head = column_block(near_values, which_head, head_size)
        live_keys = jnp.any(block_hit & block_live[which_head][:, None], axis=0)
        scores = contract_cols(query_head, key_head) * score_scale
        scores = jnp.where(causal & live_keys[None, :], scores, -jnp.inf)
        row_max = jnp.max(scores, axis=1)
        raw_weights = jnp.exp(scores - row_max[:, None])
        row_sum = jnp.sum(raw_weights, axis=1)
        weights = (raw_weights / row_sum[:, None]).astype(bf16)
        head_out = jnp.dot(weights, value_head, preferred_element_type=f32).astype(bf16)
        return (
            place_cols(context, head_out, which_head, head_size),
            weight_store.at[which_head].set(weights),
            max_store.at[which_head].set(row_max),
            sum_store.at[which_head].set(row_sum),
        )

    start_buffers = (
        jnp.zeros((tok_rows, row_width), bf16),
        jnp.zeros((local_heads, tok_rows, key_count), bf16),
        jnp.zeros((local_heads, tok_rows), f32),
        jnp.zeros((local_heads, tok_rows), f32),
    )
    context, weight_store, max_store, sum_store = lax.fori_loop(
        0, local_heads, forward_head, start_buffers
    )
    context_f = context.astype(f32)
    squares = lax.psum(jnp.sum(context_f * context_f, axis=1), "head")
    inverse = lax.rsqrt(squares / D + EPSILON)
    normed = (context_f * inverse[:, None] * norm_gain[None, :]).astype(bf16)
    out_f = out_grad.astype(f32)
    scaled_grad = norm_gain[None, :] * out_f
    correction = lax.psum(jnp.sum(scaled_grad * context_f, axis=1), "head")
    context_grad = (
        inverse[:, None] * scaled_grad
        - (inverse * inverse * inverse * correction / D)[:, None] * context_f
    ).astype(bf16)
    gain_local = jnp.sum(out_f * context_f * inverse[:, None], axis=0)
    gain_grad = lax.psum(gain_local, "seq") / math.sqrt(seq_devices * tok_rows)
    out_dots = jnp.sum(
        (context_grad.astype(f32) * context_f).reshape(tok_rows, local_heads, head_size), axis=2
    ).T
    far_rows = key_count - tok_rows

    def backward_head(which_head, buffers):
        query_grad, key_near, value_near, key_far, value_far = buffers
        query_head = column_block(queries, which_head, head_size)
        key_head = column_block(near_keys, which_head, head_size)
        value_head = column_block(near_values, which_head, head_size)
        grad_head = column_block(context_grad, which_head, head_size)
        weights = weight_store[which_head]
        weight_grad = contract_cols(grad_head, value_head)
        score_grad = (
            weights.astype(f32) * (weight_grad - out_dots[which_head][:, None]) * score_scale
        ).astype(bf16)
        query_grad = place_cols(
            query_grad,
            jnp.dot(score_grad, key_head, preferred_element_type=f32).astype(bf16),
            which_head,
            head_size,
        )
        key_terms = contract_rows(score_grad, query_head)
        value_terms = contract_rows(weights, grad_head)
        key_near = place_cols(key_near, key_terms[:tok_rows], which_head, head_size)
        value_near = place_cols(value_near, value_terms[:tok_rows], which_head, head_size)
        key_far = place_cols(key_far, key_terms[tok_rows:].astype(bf16), which_head, head_size)
        value_far = place_cols(
            value_far, value_terms[tok_rows:].astype(bf16), which_head, head_size
        )
        return (query_grad, key_near, value_near, key_far, value_far)

    start_grads = (
        jnp.zeros((tok_rows, row_width), bf16),
        jnp.zeros((tok_rows, row_width), f32),
        jnp.zeros((tok_rows, row_width), f32),
        jnp.zeros((far_rows, row_width), bf16),
        jnp.zeros((far_rows, row_width), bf16),
    )
    query_grad, key_total, value_total, key_far, value_far = lax.fori_loop(
        0, local_heads, backward_head, start_grads
    )
    for exponent in range(level_count):
        first_row = exponent * tok_rows
        back_keys, back_values = shifted(
            (
                key_far[first_row : first_row + tok_rows],
                value_far[first_row : first_row + tok_rows],
            ),
            "seq",
            -(2**exponent),
        )
        key_total = key_total + back_keys.astype(f32)
        value_total = value_total + back_values.astype(f32)
    return (normed, query_grad, key_total.astype(bf16), value_total.astype(bf16), gain_grad)


def solution(mesh):
    placed = (
        P("seq", "head"),
        P("seq", "head"),
        P("seq", "head"),
        P("seq", "head"),
        P("head"),
        P("head", None),
    )
    return jax.shard_map(
        body,
        mesh=mesh,
        in_specs=placed,
        out_specs=(
            P("seq", "head"),
            P("seq", "head"),
            P("seq", "head"),
            P("seq", "head"),
            P("head"),
        ),
        check_vma=False,
    )
```

profile of v0, /device:TPU:78, one launch (start us, length us, event | category | flops | bytes accessed | tf_op | source)
XLA Modules:
  0.0 562.6 jit_solution(15485828811725810289)
XLA Ops:
  3.4 4.5 collective-permute-start.2
  7.9 4.7 collective-permute-start.1
  18.0 5.1 collective-permute-done
  23.1 11.6 %collective-permute-start.3 = (bf16[128,1024]{1,0:T(8,128)(2,1)}, bf16[128,1024]{1,0:T(8,128)(2,1)S(1)}, u32[]{:S(2)}, u32[]{:S(2)}) collective-permute-start(bf16[128,1024]{1,0:T(8,128)(2,1)} %param.13), channel_id=1, source_target_pairs={{0,32},{4,36},{8,40},{12,44},{16,48},{20,52},{24,56},{28,60},{32,6... | collective-permute-start | bytes 786440 | tf_op jit(solution)/shard_map/ppermute | solution.py:15
  40.4 8.0 %collective-permute-done.3 = bf16[128,1024]{1,0:T(8,128)(2,1)S(1)} collective-permute-done((bf16[128,1024]{1,0:T(8,128)(2,1)}, bf16[128,1024]{1,0:T(8,128)(2,1)S(1)}, u32[]{:S(2)}, u32[]{:S(2)}) %collective-permute-start.3) | collective-permute-done | bytes 262176 | tf_op jit(solution)/shard_map/ppermute | solution.py:15
  53.1 4.5 collective-permute-start.8
  63.4 12.0 %collective-permute-done.8 = bf16[128,1024]{1,0:T(8,128)(2,1)S(1)} collective-permute-done((bf16[128,1024]{1,0:T(8,128)(2,1)S(1)}, bf16[128,1024]{1,0:T(8,128)(2,1)S(1)}, u32[]{:S(2)}, u32[]{:S(2)}) %collective-permute-start.8) | collective-permute-done | bytes 262176 | tf_op jit(solution)/shard_map/ppermute | solution.py:15
  76.7 11.6 %collective-permute-done.9 = bf16[128,1024]{1,0:T(8,128)(2,1)S(1)} collective-permute-done((bf16[128,1024]{1,0:T(8,128)(2,1)S(1)}, bf16[128,1024]{1,0:T(8,128)(2,1)S(1)}, u32[]{:S(2)}, u32[]{:S(2)}) %collective-permute-start.9) | collective-permute-done | bytes 262176 | tf_op jit(solution)/shard_map/ppermute | solution.py:15
  88.4 5.2 collective-permute-done.13
  95.3 36.2 %while.39 = (s32[]{:T(128)}, bf16[128,1024]{1,0:T(8,128)(2,1)S(1)}, bf16[8,128,1024]{2,1,0:T(8,128)(2,1)S(1)}, pred[8,8]{1,0:T(8,128)(4,1)S(1)}, bf16[128,1024]{...) while((s32[]{:T(128)}, bf16[128,1024]{1,0:T(8,128)(2,1)S(1)}, ...), condition=%wide.region_5.6_spmd.clone, body=%wide.region_0.5_spmd.clone.sunk | while | flops 69114640 | bytes 3228417 | solution.py:89
  131.7 16.8 %psum.21 = f32[128]{0:T(128)S(1)} all-reduce(f32[128]{0:T(128)S(1)} %fusion.40), channel_id=1, replica_groups=mesh['seq'=128,'head'=4] {'head'}, use_global_device_ids=true, to_apply=%region_7.8 | all-reduce | flops 128 | bytes 1024 | tf_op jit(solution)/shard_map/psum | solution.py:93
  148.6 9.2 %psum.22 = f32[128]{0:T(128)S(1)} all-reduce(f32[128]{0:T(128)S(1)} %get-tuple-element.443), channel_id=1, replica_groups=mesh['seq'=128,'head'=4] {'head'}, use_global_device_ids=true, to_apply=%region_9.10 | all-reduce | flops 128 | bytes 1024 | tf_op jit(solution)/shard_map/psum | solution.py:98
  162.9 41.5 %while.38 = (s32[]{:T(128)}, bf16[128,1024]{1,0:T(8,128)(2,1)}, f32[128,1024]{1,0:T(8,128)S(1)}, f32[128,1024]{1,0:T(8,128)S(1)}, bf16[896,1024]{1,0:T(8,128)(2,...) while((s32[]{:T(128)}, bf16[128,1024]{1,0:T(8,128)(2,1)}, ...), condition=%wide.region_12.13_spmd, body=%wide.region_11.12_spmd.sunk | while | flops 134889472 | bytes 4198627 | solution.py:144
  208.1 7.9 %collective-permute-start.27 = (bf16[128,1024]{1,0:T(8,128)(2,1)S(1)}, bf16[128,1024]{1,0:T(8,128)(2,1)S(1)}, u32[]{:S(2)}, u32[]{:S(2)}) collective-permute-start(bf16[128,1024]{1,0:T(8,128)(2,1)S(1)} %get-tuple-element.497), channel_id=1, source_target_pairs={{256,0},{260,4},{264,8},{268,12},{272,16},{276,20},{280,24},{284,2... | collective-permute-start | bytes 786440 | tf_op jit(solution)/shard_map/ppermute | solution.py:15
  217.3 4.3 collective-permute-start.25
  224.5 2.9 collective-permute-start.23
  227.4 5.6 collective-permute-start.22
  233.0 2.9 collective-permute-start.14
  235.9 3.2 collective-permute-start.20
  239.2 242.2 %psum.23 = f32[1024]{0:T(1024)S(1)} all-reduce(f32[1024]{0:T(1024)S(1)} %get-tuple-element.442), channel_id=1, replica_groups=mesh['seq'=128,'head'=4] {'seq'}, use_global_device_ids=true, to_apply=%region_14.15 | all-reduce | flops 1024 | bytes 8192 | tf_op jit(solution)/shard_map/psum | solution.py:104
  484.7 44.5 %collective-permute-start.18 = (bf16[128,1024]{1,0:T(8,128)(2,1)S(1)}, bf16[128,1024]{1,0:T(8,128)(2,1)S(1)}, u32[]{:S(2)}, u32[]{:S(2)}) collective-permute-start(bf16[128,1024]{1,0:T(8,128)(2,1)S(1)} %get-tuple-element.506), channel_id=1, source_target_pairs={{64,0},{68,4},{72,8},{76,12},{80,16},{84,20},{88,24},{92,28},{96,3... | collective-permute-start | bytes 786440 | tf_op jit(solution)/shard_map/ppermute | solution.py:15
  533.9 7.6 %collective-permute-start.15 = (bf16[128,1024]{1,0:T(8,128)(2,1)S(1)}, bf16[128,1024]{1,0:T(8,128)(2,1)S(1)}, u32[]{:S(2)}, u32[]{:S(2)}) collective-permute-start(bf16[128,1024]{1,0:T(8,128)(2,1)S(1)} %get-tuple-element.509), channel_id=1, source_target_pairs={{8,0},{12,4},{16,8},{20,12},{24,16},{28,20},{32,24},{36,28},{40,32... | collective-permute-start | bytes 786440 | tf_op jit(solution)/shard_map/ppermute | solution.py:15
  544.6 6.6 %collective-permute-done.16 = bf16[128,1024]{1,0:T(8,128)(2,1)S(1)} collective-permute-done((bf16[128,1024]{1,0:T(8,128)(2,1)S(1)}, bf16[128,1024]{1,0:T(8,128)(2,1)S(1)}, u32[]{:S(2)}, u32[]{:S(2)}) %collective-permute-start.16) | collective-permute-done | bytes 262176 | tf_op jit(solution)/shard_map/ppermute | solution.py:15
  551.2 9.3 %collective-permute-done.15 = bf16[128,1024]{1,0:T(8,128)(2,1)S(1)} collective-permute-done((bf16[128,1024]{1,0:T(8,128)(2,1)S(1)}, bf16[128,1024]{1,0:T(8,128)(2,1)S(1)}, u32[]{:S(2)}, u32[]{:S(2)}) %collective-permute-start.15) | collective-permute-done | bytes 262176 | tf_op jit(solution)/shard_map/ppermute | solution.py:15
  (210 shorter events, 130.8 us)
Async XLA Ops:
  0.6 52.5 %collective-permute-start.5 = (bf16[128,1024]{1,0:T(8,128)(2,1)}, bf16[128,1024]{1,0:T(8,128)(2,1)S(1)}, u32[]{:S(2)}, u32[]{:S(2)}) collective-permute-start(bf16[128,1024]{1,0:T(8,128)(2,1)} %param.13), channel_id=1, source_target_pairs={{0,128},{4,132},{8,136},{12,140},{16,144},{20,148},{24,152},{28,15... | collective-permute-start | bytes 786440 | tf_op jit(solution)/shard_map/ppermute | solution.py:15
  2.1 48.4 %collective-permute-start.4 = (bf16[128,1024]{1,0:T(8,128)(2,1)}, bf16[128,1024]{1,0:T(8,128)(2,1)S(1)}, u32[]{:S(2)}, u32[]{:S(2)}) collective-permute-start(bf16[128,1024]{1,0:T(8,128)(2,1)} %param.13), channel_id=1, source_target_pairs={{0,64},{4,68},{8,72},{12,76},{16,80},{20,84},{24,88},{28,92},{32,9... | collective-permute-start | bytes 786440 | tf_op jit(solution)/shard_map/ppermute | solution.py:15
  3.4 35.0 %collective-permute-start.2 = (bf16[128,1024]{1,0:T(8,128)(2,1)}, bf16[128,1024]{1,0:T(8,128)(2,1)S(1)}, u32[]{:S(2)}, u32[]{:S(2)}) collective-permute-start(bf16[128,1024]{1,0:T(8,128)(2,1)} %param.13), channel_id=1, source_target_pairs={{0,16},{4,20},{8,24},{12,28},{16,32},{20,36},{24,40},{28,44},{32,4... | collective-permute-start | bytes 786440 | tf_op jit(solution)/shard_map/ppermute | solution.py:15
  7.9 28.5 %collective-permute-start.1 = (bf16[128,1024]{1,0:T(8,128)(2,1)}, bf16[128,1024]{1,0:T(8,128)(2,1)S(1)}, u32[]{:S(2)}, u32[]{:S(2)}) collective-permute-start(bf16[128,1024]{1,0:T(8,128)(2,1)} %param.13), channel_id=1, source_target_pairs={{0,8},{4,12},{8,16},{12,20},{16,24},{20,28},{24,32},{28,36},{32,40... | collective-permute-start | bytes 786440 | tf_op jit(solution)/shard_map/ppermute | solution.py:15
  23.1 25.3 %collective-permute-start.3 = (bf16[128,1024]{1,0:T(8,128)(2,1)}, bf16[128,1024]{1,0:T(8,128)(2,1)S(1)}, u32[]{:S(2)}, u32[]{:S(2)}) collective-permute-start(bf16[128,1024]{1,0:T(8,128)(2,1)} %param.13), channel_id=1, source_target_pairs={{0,32},{4,36},{8,40},{12,44},{16,48},{20,52},{24,56},{28,60},{32,6... | collective-permute-start | bytes 786440 | tf_op jit(solution)/shard_map/ppermute | solution.py:15
  36.4 22.0 %collective-permute-start.6 = (bf16[128,1024]{1,0:T(8,128)(2,1)}, bf16[128,1024]{1,0:T(8,128)(2,1)S(1)}, u32[]{:S(2)}, u32[]{:S(2)}) collective-permute-start(bf16[128,1024]{1,0:T(8,128)(2,1)} %param.13), channel_id=1, source_target_pairs={{0,256},{4,260},{8,264},{12,268},{16,272},{20,276},{24,280},{28,28... | collective-permute-start | bytes 786440 | tf_op jit(solution)/shard_map/ppermute | solution.py:15
  38.4 50.0 %collective-permute-start.12 = (bf16[128,1024]{1,0:T(8,128)(2,1)S(1)}, bf16[128,1024]{1,0:T(8,128)(2,1)S(1)}, u32[]{:S(2)}, u32[]{:S(2)}) collective-permute-start(bf16[128,1024]{1,0:T(8,128)(2,1)S(1)} %copy-done.7), channel_id=1, source_target_pairs={{0,128},{4,132},{8,136},{12,140},{16,144},{20,148},{24,152},{28,15... | collective-permute-start | bytes 786440 | tf_op jit(solution)/shard_map/ppermute | solution.py:15
  48.4 39.9 %collective-permute-start.11 = (bf16[128,1024]{1,0:T(8,128)(2,1)S(1)}, bf16[128,1024]{1,0:T(8,128)(2,1)S(1)}, u32[]{:S(2)}, u32[]{:S(2)}) collective-permute-start(bf16[128,1024]{1,0:T(8,128)(2,1)S(1)} %copy-done.7), channel_id=1, source_target_pairs={{0,64},{4,68},{8,72},{12,76},{16,80},{20,84},{24,88},{28,92},{32,9... | collective-permute-start | bytes 786440 | tf_op jit(solution)/shard_map/ppermute | solution.py:15
  53.1 22.3 %collective-permute-start.8 = (bf16[128,1024]{1,0:T(8,128)(2,1)S(1)}, bf16[128,1024]{1,0:T(8,128)(2,1)S(1)}, u32[]{:S(2)}, u32[]{:S(2)}) collective-permute-start(bf16[128,1024]{1,0:T(8,128)(2,1)S(1)} %copy-done.7), channel_id=1, source_target_pairs={{0,8},{4,12},{8,16},{12,20},{16,24},{20,28},{24,32},{28,36},{32,40... | collective-permute-start | bytes 786440 | tf_op jit(solution)/shard_map/ppermute | solution.py:15
  58.4 29.9 %collective-permute-start.9 = (bf16[128,1024]{1,0:T(8,128)(2,1)S(1)}, bf16[128,1024]{1,0:T(8,128)(2,1)S(1)}, u32[]{:S(2)}, u32[]{:S(2)}) collective-permute-start(bf16[128,1024]{1,0:T(8,128)(2,1)S(1)} %copy-done.7), channel_id=1, source_target_pairs={{0,16},{4,20},{8,24},{12,28},{16,32},{20,36},{24,40},{28,44},{32,4... | collective-permute-start | bytes 786440 | tf_op jit(solution)/shard_map/ppermute | solution.py:15
  61.4 26.9 %collective-permute-start.10 = (bf16[128,1024]{1,0:T(8,128)(2,1)S(1)}, bf16[128,1024]{1,0:T(8,128)(2,1)S(1)}, u32[]{:S(2)}, u32[]{:S(2)}) collective-permute-start(bf16[128,1024]{1,0:T(8,128)(2,1)S(1)} %copy-done.7), channel_id=1, source_target_pairs={{0,32},{4,36},{8,40},{12,44},{16,48},{20,52},{24,56},{28,60},{32,6... | collective-permute-start | bytes 786440 | tf_op jit(solution)/shard_map/ppermute | solution.py:15
  75.4 18.3 %collective-permute-start.13 = (bf16[128,1024]{1,0:T(8,128)(2,1)S(1)}, bf16[128,1024]{1,0:T(8,128)(2,1)S(1)}, u32[]{:S(2)}, u32[]{:S(2)}) collective-permute-start(bf16[128,1024]{1,0:T(8,128)(2,1)S(1)} %copy-done.7), channel_id=1, source_target_pairs={{0,256},{4,260},{8,264},{12,268},{16,272},{20,276},{24,280},{28,28... | collective-permute-start | bytes 786440 | tf_op jit(solution)/shard_map/ppermute | solution.py:15
  206.2 18.3 %collective-permute-start.21 = (bf16[128,1024]{1,0:T(8,128)(2,1)S(1)}, bf16[128,1024]{1,0:T(8,128)(2,1)S(1)}, u32[]{:S(2)}, u32[]{:S(2)}) collective-permute-start(bf16[128,1024]{1,0:T(8,128)(2,1)S(1)} %get-tuple-element.496), channel_id=1, source_target_pairs={{4,0},{8,4},{12,8},{16,12},{20,16},{24,20},{28,24},{32,28},{36,32}... | collective-permute-start | bytes 786440 | tf_op jit(solution)/shard_map/ppermute | solution.py:15
  208.1 19.3 %collective-permute-start.27 = (bf16[128,1024]{1,0:T(8,128)(2,1)S(1)}, bf16[128,1024]{1,0:T(8,128)(2,1)S(1)}, u32[]{:S(2)}, u32[]{:S(2)}) collective-permute-start(bf16[128,1024]{1,0:T(8,128)(2,1)S(1)} %get-tuple-element.497), channel_id=1, source_target_pairs={{256,0},{260,4},{264,8},{268,12},{272,16},{276,20},{280,24},{284,2... | collective-permute-start | bytes 786440 | tf_op jit(solution)/shard_map/ppermute | solution.py:15
  217.3 18.6 %collective-permute-start.25 = (bf16[128,1024]{1,0:T(8,128)(2,1)S(1)}, bf16[128,1024]{1,0:T(8,128)(2,1)S(1)}, u32[]{:S(2)}, u32[]{:S(2)}) collective-permute-start(bf16[128,1024]{1,0:T(8,128)(2,1)S(1)} %get-tuple-element.499), channel_id=1, source_target_pairs={{64,0},{68,4},{72,8},{76,12},{80,16},{84,20},{88,24},{92,28},{96,3... | collective-permute-start | bytes 786440 | tf_op jit(solution)/shard_map/ppermute | solution.py:15
  221.6 260.3 %collective-permute-start.24 = (bf16[128,1024]{1,0:T(8,128)(2,1)S(1)}, bf16[128,1024]{1,0:T(8,128)(2,1)}, u32[]{:S(2)}, u32[]{:S(2)}) collective-permute-start(bf16[128,1024]{1,0:T(8,128)(2,1)S(1)} %get-tuple-element.500), channel_id=1, source_target_pairs={{32,0},{36,4},{40,8},{44,12},{48,16},{52,20},{56,24},{60,28},{64,3... | collective-permute-start | bytes 786440 | tf_op jit(solution)/shard_map/ppermute | solution.py:15
  224.5 260.2 %collective-permute-start.23 = (bf16[128,1024]{1,0:T(8,128)(2,1)S(1)}, bf16[128,1024]{1,0:T(8,128)(2,1)}, u32[]{:S(2)}, u32[]{:S(2)}) collective-permute-start(bf16[128,1024]{1,0:T(8,128)(2,1)S(1)} %get-tuple-element.501), channel_id=1, source_target_pairs={{16,0},{20,4},{24,8},{28,12},{32,16},{36,20},{40,24},{44,28},{48,3... | collective-permute-start | bytes 786440 | tf_op jit(solution)/shard_map/ppermute | solution.py:15
  227.4 301.8 %collective-permute-start.22 = (bf16[128,1024]{1,0:T(8,128)(2,1)S(1)}, bf16[128,1024]{1,0:T(8,128)(2,1)}, u32[]{:S(2)}, u32[]{:S(2)}) collective-permute-start(bf16[128,1024]{1,0:T(8,128)(2,1)S(1)} %get-tuple-element.502), channel_id=1, source_target_pairs={{8,0},{12,4},{16,8},{20,12},{24,16},{28,20},{32,24},{36,28},{40,32... | collective-permute-start | bytes 786440 | tf_op jit(solution)/shard_map/ppermute | solution.py:15
  233.0 298.1 %collective-permute-start.14 = (bf16[128,1024]{1,0:T(8,128)(2,1)}, bf16[128,1024]{1,0:T(8,128)(2,1)}, u32[]{:S(2)}, u32[]{:S(2)}) collective-permute-start(bf16[128,1024]{1,0:T(8,128)(2,1)} %get-tuple-element.503), channel_id=1, source_target_pairs={{4,0},{8,4},{12,8},{16,12},{20,16},{24,20},{28,24},{32,28},{36,32}... | collective-permute-start | bytes 786440 | tf_op jit(solution)/shard_map/ppermute | solution.py:15
  235.9 298.0 %collective-permute-start.20 = (bf16[128,1024]{1,0:T(8,128)(2,1)S(1)}, bf16[128,1024]{1,0:T(8,128)(2,1)}, u32[]{:S(2)}, u32[]{:S(2)}) collective-permute-start(bf16[128,1024]{1,0:T(8,128)(2,1)S(1)} %get-tuple-element.504), channel_id=1, source_target_pairs={{256,0},{260,4},{264,8},{268,12},{272,16},{276,20},{280,24},{284,2... | collective-permute-start | bytes 786440 | tf_op jit(solution)/shard_map/ppermute | solution.py:15
  481.9 62.0 %collective-permute-start.19 = (bf16[128,1024]{1,0:T(8,128)(2,1)S(1)}, bf16[128,1024]{1,0:T(8,128)(2,1)S(1)}, u32[]{:S(2)}, u32[]{:S(2)}) collective-permute-start(bf16[128,1024]{1,0:T(8,128)(2,1)S(1)} %get-tuple-element.505), channel_id=1, source_target_pairs={{128,0},{132,4},{136,8},{140,12},{144,16},{148,20},{152,24},{156,2... | collective-permute-start | bytes 786440 | tf_op jit(solution)/shard_map/ppermute | solution.py:15
  484.7 59.3 %collective-permute-start.18 = (bf16[128,1024]{1,0:T(8,128)(2,1)S(1)}, bf16[128,1024]{1,0:T(8,128)(2,1)S(1)}, u32[]{:S(2)}, u32[]{:S(2)}) collective-permute-start(bf16[128,1024]{1,0:T(8,128)(2,1)S(1)} %get-tuple-element.506), channel_id=1, source_target_pairs={{64,0},{68,4},{72,8},{76,12},{80,16},{84,20},{88,24},{92,28},{96,3... | collective-permute-start | bytes 786440 | tf_op jit(solution)/shard_map/ppermute | solution.py:15
  531.2 20.1 %collective-permute-start.16 = (bf16[128,1024]{1,0:T(8,128)(2,1)S(1)}, bf16[128,1024]{1,0:T(8,128)(2,1)S(1)}, u32[]{:S(2)}, u32[]{:S(2)}) collective-permute-start(bf16[128,1024]{1,0:T(8,128)(2,1)S(1)} %get-tuple-element.508), channel_id=1, source_target_pairs={{16,0},{20,4},{24,8},{28,12},{32,16},{36,20},{40,24},{44,28},{48,3... | collective-permute-start | bytes 786440 | tf_op jit(solution)/shard_map/ppermute | solution.py:15
  533.9 26.7 %collective-permute-start.15 = (bf16[128,1024]{1,0:T(8,128)(2,1)S(1)}, bf16[128,1024]{1,0:T(8,128)(2,1)S(1)}, u32[]{:S(2)}, u32[]{:S(2)}) collective-permute-start(bf16[128,1024]{1,0:T(8,128)(2,1)S(1)} %get-tuple-element.509), channel_id=1, source_target_pairs={{8,0},{12,4},{16,8},{20,12},{24,16},{28,20},{32,24},{36,28},{40,32... | collective-permute-start | bytes 786440 | tf_op jit(solution)/shard_map/ppermute | solution.py:15
  (14 other events, 261.3 us)
where the time goes:
time: 565 us; the launch traced here: 563 us
  blocking collectives  268 us (47%)
  starting transfers between devices  133 us (24%)
  waiting for transfers between devices  58.6 us (10%)
  matrix products  54.5 us (10%)
  local copies, waits for them, and re-layouts  24.5 us (4%)
  other arithmetic  22.6 us (4%)
    psum x1, blocking collectives, body(): gain_grad = lax.psum(gain_local, 'seq') / math.sqrt(seq_devices * tok_rows)  242 us
    ppermute x28, starting transfers between devices, shifted(): return lax.ppermute(x, axis, pairs)  133 us
    ppermute x28, waiting for transfers between devices, shifted(): return lax.ppermute(x, axis, pairs)  58.6 us
    dot_general x16, matrix products, contract_cols(): lax.dot_general(left_side, right_side, (((1,), (1,)), ((), ())), preferre...  19.9 us
    psum x1, blocking collectives, body(): squares = lax.psum(jnp.sum(context_f * context_f, axis=1), 'head')  16.8 us
    dot_general x8, matrix products, backward_head(): jnp.dot(score_grad, key_head, preferred_element_type=f32).astype(bf16)  14.4 us
  transfers between devices with their start and end apart: 28, of which 8 were waited for; matrix products, arithmetic and copies ran while one was open for 2% of the time, Pallas kernels for 0%

commit v1 on v0

--- a/solution.py
+++ b/solution.py
@@ -101,7 +101,9 @@
         - (inverse * inverse * inverse * correction / D)[:, None] * context_f
     ).astype(bf16)
     gain_local = jnp.sum(out_f * context_f * inverse[:, None], axis=0)
-    gain_grad = lax.psum(gain_local, "seq") / math.sqrt(seq_devices * tok_rows)
+    gain_grad = jnp.sum(lax.all_gather(gain_local, "seq"), axis=0) / math.sqrt(
+        seq_devices * tok_rows
+    )
     out_dots = jnp.sum(
         (context_grad.astype(f32) * context_f).reshape(tok_rows, local_heads, head_size), axis=2
     ).T

time: 565 us -> 450 us (0.80)
  the two profiles are of different devices: /device:TPU:78 before, /device:TPU:73 now
where the time goes in v1:
time: 450 us; the launch traced here: 448 us
  blocking collectives  187 us (42%)
  starting transfers between devices  89.5 us (20%)
  waiting for transfers between devices  66.8 us (15%)
  matrix products  54.5 us (12%)
  local copies, waits for them, and re-layouts  25.5 us (6%)
  other arithmetic  22.7 us (5%)
    all_gather x1, blocking collectives, body(): lax.all_gather(gain_local, 'seq')  165 us
    ppermute x28, starting transfers between devices, shifted(): return lax.ppermute(x, axis, pairs)  89.5 us
    ppermute x28, waiting for transfers between devices, shifted(): return lax.ppermute(x, axis, pairs)  66.8 us
    dot_general x16, matrix products, contract_cols(): lax.dot_general(left_side, right_side, (((1,), (1,)), ((), ())), preferre...  19.9 us
    psum x1, blocking collectives, body(): squares = lax.psum(jnp.sum(context_f * context_f, axis=1), 'head')  14.7 us
    dot_general x8, matrix products, backward_head(): jnp.dot(score_grad, key_head, preferred_element_type=f32).astype(bf16)  14.4 us
    dot_general x16, matrix products, contract_rows(): lax.dot_general(left_side, right_side, (((0,), (0,)), ((), ())), preferre...  10.1 us
    dot_general x8, matrix products, forward_head(): jnp.dot(weights, value_head, preferred_element_type=f32).astype(bf16)  10.1 us
  transfers between devices with their start and end apart: 28, of which 6 were waited for; matrix products, arithmetic and copies ran while one was open for 3% of the time, Pallas kernels for 0%

profile of v1, /device:TPU:73, one launch (start us, length us, event | category | flops | bytes accessed | tf_op | source)
XLA Modules:
  0.0 447.6 jit_solution(14391629522307609574)
XLA Ops:
  0.6 4.8 %collective-permute-start.5 = (bf16[128,1024]{1,0:T(8,128)(2,1)}, bf16[128,1024]{1,0:T(8,128)(2,1)S(1)}, u32[]{:S(2)}, u32[]{:S(2)}) collective-permute-start(bf16[128,1024]{1,0:T(8,128)(2,1)} %param.13), channel_id=1, source_target_pairs={{0,128},{4,132},{8,136},{12,140},{16,144},{20,148},{24,152},{28,15... | collective-permute-start | bytes 786440 | tf_op jit(solution)/shard_map/ppermute | solution.py:15
  7.7 4.2 collective-permute-start.2
  11.9 4.4 collective-permute-start.1
  16.3 4.0 collective-permute-start
  23.8 8.5 %collective-permute-done = bf16[128,1024]{1,0:T(8,128)(2,1)} collective-permute-done((bf16[128,1024]{1,0:T(8,128)(2,1)}, bf16[128,1024]{1,0:T(8,128)(2,1)}, u32[]{:S(2)}, u32[]{:S(2)}) %collective-permute-start) | collective-permute-done | bytes 262176 | tf_op jit(solution)/shard_map/ppermute | solution.py:15
  32.3 4.9 %collective-permute-start.3 = (bf16[128,1024]{1,0:T(8,128)(2,1)}, bf16[128,1024]{1,0:T(8,128)(2,1)S(1)}, u32[]{:S(2)}, u32[]{:S(2)}) collective-permute-start(bf16[128,1024]{1,0:T(8,128)(2,1)} %param.13), channel_id=1, source_target_pairs={{0,32},{4,36},{8,40},{12,44},{16,48},{20,52},{24,56},{28,60},{32,6... | collective-permute-start | bytes 786440 | tf_op jit(solution)/shard_map/ppermute | solution.py:15
  43.5 6.8 %collective-permute-done.3 = bf16[128,1024]{1,0:T(8,128)(2,1)S(1)} collective-permute-done((bf16[128,1024]{1,0:T(8,128)(2,1)}, bf16[128,1024]{1,0:T(8,128)(2,1)S(1)}, u32[]{:S(2)}, u32[]{:S(2)}) %collective-permute-start.3) | collective-permute-done | bytes 262176 | tf_op jit(solution)/shard_map/ppermute | solution.py:15
  53.0 8.7 %collective-permute-start.7 = (bf16[128,1024]{1,0:T(8,128)(2,1)S(1)}, bf16[128,1024]{1,0:T(8,128)(2,1)S(1)}, u32[]{:S(2)}, u32[]{:S(2)}) collective-permute-start(bf16[128,1024]{1,0:T(8,128)(2,1)S(1)} %copy-done.7), channel_id=1, source_target_pairs={{0,4},{4,8},{8,12},{12,16},{16,20},{20,24},{24,28},{28,32},{32,36}... | collective-permute-start | bytes 786440 | tf_op jit(solution)/shard_map/ppermute | solution.py:15
  62.4 4.3 collective-permute-start.8
  72.0 3.5 collective-permute-done.8
  76.8 23.5 %collective-permute-done.9 = bf16[128,1024]{1,0:T(8,128)(2,1)S(1)} collective-permute-done((bf16[128,1024]{1,0:T(8,128)(2,1)S(1)}, bf16[128,1024]{1,0:T(8,128)(2,1)S(1)}, u32[]{:S(2)}, u32[]{:S(2)}) %collective-permute-start.9) | collective-permute-done | bytes 262176 | tf_op jit(solution)/shard_map/ppermute | solution.py:15
  102.1 36.2 %while.39 = (s32[]{:T(128)}, bf16[128,1024]{1,0:T(8,128)(2,1)S(1)}, bf16[8,128,1024]{2,1,0:T(8,128)(2,1)S(1)}, pred[8,8]{1,0:T(8,128)(4,1)S(1)}, bf16[128,1024]{...) while((s32[]{:T(128)}, bf16[128,1024]{1,0:T(8,128)(2,1)S(1)}, ...), condition=%wide.region_5.6_spmd.clone, body=%wide.region_0.5_spmd.clone.sunk | while | flops 69114640 | bytes 3228417 | solution.py:89
  138.5 14.7 %psum.14 = f32[128]{0:T(128)S(1)} all-reduce(f32[128]{0:T(128)S(1)} %fusion.40), channel_id=1, replica_groups=mesh['seq'=128,'head'=4] {'head'}, use_global_device_ids=true, to_apply=%region_7.8 | all-reduce | flops 128 | bytes 1024 | tf_op jit(solution)/shard_map/psum | solution.py:93
  153.4 7.4 %psum.15 = f32[128]{0:T(128)S(1)} all-reduce(f32[128]{0:T(128)S(1)} %get-tuple-element.443), channel_id=1, replica_groups=mesh['seq'=128,'head'=4] {'head'}, use_global_device_ids=true, to_apply=%region_9.10 | all-reduce | flops 128 | bytes 1024 | tf_op jit(solution)/shard_map/psum | solution.py:98
  166.0 41.5 %while.38 = (s32[]{:T(128)}, bf16[128,1024]{1,0:T(8,128)(2,1)}, f32[128,1024]{1,0:T(8,128)S(1)}, f32[128,1024]{1,0:T(8,128)S(1)}, bf16[896,1024]{1,0:T(8,128)(2,...) while((s32[]{:T(128)}, bf16[128,1024]{1,0:T(8,128)(2,1)}, ...), condition=%wide.region_12.13_spmd, body=%wide.region_11.12_spmd.sunk | while | flops 134889472 | bytes 4198627 | solution.py:146
  210.0 6.6 %collective-permute-start.21 = (bf16[128,1024]{1,0:T(8,128)(2,1)S(1)}, bf16[128,1024]{1,0:T(8,128)(2,1)S(1)}, u32[]{:S(2)}, u32[]{:S(2)}) collective-permute-start(bf16[128,1024]{1,0:T(8,128)(2,1)S(1)} %get-tuple-element.496), channel_id=1, source_target_pairs={{4,0},{8,4},{12,8},{16,12},{20,16},{24,20},{28,24},{32,28},{36,32}... | collective-permute-start | bytes 786440 | tf_op jit(solution)/shard_map/ppermute | solution.py:15
  225.5 4.2 collective-permute-start.23
  229.7 3.3 collective-permute-start.22
  233.0 2.8 collective-permute-start.14
  237.9 164.8 %all-gather = f32[131072]{0:T(1024)S(1)} all-gather(f32[1024]{0:T(1024)S(1)} %get-tuple-element.442), channel_id=2, replica_groups=mesh['seq'=128,'head'=4] {'seq'}, dimensions={0}, use_global_device_ids=true | all-gather | bytes 528384 | tf_op jit(solution)/shard_map/all_gather | solution.py:104
  410.0 5.3 %collective-permute-start.16 = (bf16[128,1024]{1,0:T(8,128)(2,1)S(1)}, bf16[128,1024]{1,0:T(8,128)(2,1)S(1)}, u32[]{:S(2)}, u32[]{:S(2)}) collective-permute-start(bf16[128,1024]{1,0:T(8,128)(2,1)S(1)} %get-tuple-element.508), channel_id=1, source_target_pairs={{16,0},{20,4},{24,8},{28,12},{32,16},{36,20},{40,24},{44,28},{48,3... | collective-permute-start | bytes 786440 | tf_op jit(solution)/shard_map/ppermute | solution.py:15
  415.3 3.2 collective-permute-start.15
  421.1 18.3 %collective-permute-done.16 = bf16[128,1024]{1,0:T(8,128)(2,1)S(1)} collective-permute-done((bf16[128,1024]{1,0:T(8,128)(2,1)S(1)}, bf16[128,1024]{1,0:T(8,128)(2,1)S(1)}, u32[]{:S(2)}, u32[]{:S(2)}) %collective-permute-start.16) | collective-permute-done | bytes 262176 | tf_op jit(solution)/shard_map/ppermute | solution.py:15
  439.4 6.2 %collective-permute-done.15 = bf16[128,1024]{1,0:T(8,128)(2,1)S(1)} collective-permute-done((bf16[128,1024]{1,0:T(8,128)(2,1)S(1)}, bf16[128,1024]{1,0:T(8,128)(2,1)S(1)}, u32[]{:S(2)}, u32[]{:S(2)}) %collective-permute-start.15) | collective-permute-done | bytes 262176 | tf_op jit(solution)/shard_map/ppermute | solution.py:15
  (212 shorter events, 131.6 us)
Async XLA Ops:
  0.6 61.7 %collective-permute-start.5 = (bf16[128,1024]{1,0:T(8,128)(2,1)}, bf16[128,1024]{1,0:T(8,128)(2,1)S(1)}, u32[]{:S(2)}, u32[]{:S(2)}) collective-permute-start(bf16[128,1024]{1,0:T(8,128)(2,1)} %param.13), channel_id=1, source_target_pairs={{0,128},{4,132},{8,136},{12,140},{16,144},{20,148},{24,152},{28,15... | collective-permute-start | bytes 786440 | tf_op jit(solution)/shard_map/ppermute | solution.py:15
  5.4 47.5 %collective-permute-start.4 = (bf16[128,1024]{1,0:T(8,128)(2,1)}, bf16[128,1024]{1,0:T(8,128)(2,1)S(1)}, u32[]{:S(2)}, u32[]{:S(2)}) collective-permute-start(bf16[128,1024]{1,0:T(8,128)(2,1)} %param.13), channel_id=1, source_target_pairs={{0,64},{4,68},{8,72},{12,76},{16,80},{20,84},{24,88},{28,92},{32,9... | collective-permute-start | bytes 786440 | tf_op jit(solution)/shard_map/ppermute | solution.py:15
  7.7 33.2 %collective-permute-start.2 = (bf16[128,1024]{1,0:T(8,128)(2,1)}, bf16[128,1024]{1,0:T(8,128)(2,1)S(1)}, u32[]{:S(2)}, u32[]{:S(2)}) collective-permute-start(bf16[128,1024]{1,0:T(8,128)(2,1)} %param.13), channel_id=1, source_target_pairs={{0,16},{4,20},{8,24},{12,28},{16,32},{20,36},{24,40},{28,44},{32,4... | collective-permute-start | bytes 786440 | tf_op jit(solution)/shard_map/ppermute | solution.py:15
  11.9 26.9 %collective-permute-start.1 = (bf16[128,1024]{1,0:T(8,128)(2,1)}, bf16[128,1024]{1,0:T(8,128)(2,1)S(1)}, u32[]{:S(2)}, u32[]{:S(2)}) collective-permute-start(bf16[128,1024]{1,0:T(8,128)(2,1)} %param.13), channel_id=1, source_target_pairs={{0,8},{4,12},{8,16},{12,20},{16,24},{20,28},{24,32},{28,36},{32,40... | collective-permute-start | bytes 786440 | tf_op jit(solution)/shard_map/ppermute | solution.py:15
  16.3 16.0 %collective-permute-start = (bf16[128,1024]{1,0:T(8,128)(2,1)}, bf16[128,1024]{1,0:T(8,128)(2,1)}, u32[]{:S(2)}, u32[]{:S(2)}) collective-permute-start(bf16[128,1024]{1,0:T(8,128)(2,1)} %param.13), channel_id=1, source_target_pairs={{0,4},{4,8},{8,12},{12,16},{16,20},{20,24},{24,28},{28,32},{32,36}... | collective-permute-start | bytes 786440 | tf_op jit(solution)/shard_map/ppermute | solution.py:15
  32.3 18.0 %collective-permute-start.3 = (bf16[128,1024]{1,0:T(8,128)(2,1)}, bf16[128,1024]{1,0:T(8,128)(2,1)S(1)}, u32[]{:S(2)}, u32[]{:S(2)}) collective-permute-start(bf16[128,1024]{1,0:T(8,128)(2,1)} %param.13), channel_id=1, source_target_pairs={{0,32},{4,36},{8,40},{12,44},{16,48},{20,52},{24,56},{28,60},{32,6... | collective-permute-start | bytes 786440 | tf_op jit(solution)/shard_map/ppermute | solution.py:15
  38.8 28.6 %collective-permute-start.6 = (bf16[128,1024]{1,0:T(8,128)(2,1)}, bf16[128,1024]{1,0:T(8,128)(2,1)S(1)}, u32[]{:S(2)}, u32[]{:S(2)}) collective-permute-start(bf16[128,1024]{1,0:T(8,128)(2,1)} %param.13), channel_id=1, source_target_pairs={{0,256},{4,260},{8,264},{12,268},{16,272},{20,276},{24,280},{28,28... | collective-permute-start | bytes 786440 | tf_op jit(solution)/shard_map/ppermute | solution.py:15
  40.9 59.5 %collective-permute-start.12 = (bf16[128,1024]{1,0:T(8,128)(2,1)S(1)}, bf16[128,1024]{1,0:T(8,128)(2,1)S(1)}, u32[]{:S(2)}, u32[]{:S(2)}) collective-permute-start(bf16[128,1024]{1,0:T(8,128)(2,1)S(1)} %copy-done.7), channel_id=1, source_target_pairs={{0,128},{4,132},{8,136},{12,140},{16,144},{20,148},{24,152},{28,15... | collective-permute-start | bytes 786440 | tf_op jit(solution)/shard_map/ppermute | solution.py:15
  50.3 50.0 %collective-permute-start.11 = (bf16[128,1024]{1,0:T(8,128)(2,1)S(1)}, bf16[128,1024]{1,0:T(8,128)(2,1)S(1)}, u32[]{:S(2)}, u32[]{:S(2)}) collective-permute-start(bf16[128,1024]{1,0:T(8,128)(2,1)S(1)} %copy-done.7), channel_id=1, source_target_pairs={{0,64},{4,68},{8,72},{12,76},{16,80},{20,84},{24,88},{28,92},{32,9... | collective-permute-start | bytes 786440 | tf_op jit(solution)/shard_map/ppermute | solution.py:15
  53.0 17.1 %collective-permute-start.7 = (bf16[128,1024]{1,0:T(8,128)(2,1)S(1)}, bf16[128,1024]{1,0:T(8,128)(2,1)S(1)}, u32[]{:S(2)}, u32[]{:S(2)}) collective-permute-start(bf16[128,1024]{1,0:T(8,128)(2,1)S(1)} %copy-done.7), channel_id=1, source_target_pairs={{0,4},{4,8},{8,12},{12,16},{16,20},{20,24},{24,28},{28,32},{32,36}... | collective-permute-start | bytes 786440 | tf_op jit(solution)/shard_map/ppermute | solution.py:15
  67.4 32.9 %collective-permute-start.9 = (bf16[128,1024]{1,0:T(8,128)(2,1)S(1)}, bf16[128,1024]{1,0:T(8,128)(2,1)S(1)}, u32[]{:S(2)}, u32[]{:S(2)}) collective-permute-start(bf16[128,1024]{1,0:T(8,128)(2,1)S(1)} %copy-done.7), channel_id=1, source_target_pairs={{0,16},{4,20},{8,24},{12,28},{16,32},{20,36},{24,40},{28,44},{32,4... | collective-permute-start | bytes 786440 | tf_op jit(solution)/shard_map/ppermute | solution.py:15
  70.0 30.3 %collective-permute-start.10 = (bf16[128,1024]{1,0:T(8,128)(2,1)S(1)}, bf16[128,1024]{1,0:T(8,128)(2,1)S(1)}, u32[]{:S(2)}, u32[]{:S(2)}) collective-permute-start(bf16[128,1024]{1,0:T(8,128)(2,1)S(1)} %copy-done.7), channel_id=1, source_target_pairs={{0,32},{4,36},{8,40},{12,44},{16,48},{20,52},{24,56},{28,60},{32,6... | collective-permute-start | bytes 786440 | tf_op jit(solution)/shard_map/ppermute | solution.py:15
  75.4 25.0 %collective-permute-start.13 = (bf16[128,1024]{1,0:T(8,128)(2,1)S(1)}, bf16[128,1024]{1,0:T(8,128)(2,1)S(1)}, u32[]{:S(2)}, u32[]{:S(2)}) collective-permute-start(bf16[128,1024]{1,0:T(8,128)(2,1)S(1)} %copy-done.7), channel_id=1, source_target_pairs={{0,256},{4,260},{8,264},{12,268},{16,272},{20,276},{24,280},{28,28... | collective-permute-start | bytes 786440 | tf_op jit(solution)/shard_map/ppermute | solution.py:15
  210.0 15.5 %collective-permute-start.21 = (bf16[128,1024]{1,0:T(8,128)(2,1)S(1)}, bf16[128,1024]{1,0:T(8,128)(2,1)S(1)}, u32[]{:S(2)}, u32[]{:S(2)}) collective-permute-start(bf16[128,1024]{1,0:T(8,128)(2,1)S(1)} %get-tuple-element.496), channel_id=1, source_target_pairs={{4,0},{8,4},{12,8},{16,12},{20,16},{24,20},{28,24},{32,28},{36,32}... | collective-permute-start | bytes 786440 | tf_op jit(solution)/shard_map/ppermute | solution.py:15
  219.8 16.0 %collective-permute-start.25 = (bf16[128,1024]{1,0:T(8,128)(2,1)S(1)}, bf16[128,1024]{1,0:T(8,128)(2,1)S(1)}, u32[]{:S(2)}, u32[]{:S(2)}) collective-permute-start(bf16[128,1024]{1,0:T(8,128)(2,1)S(1)} %get-tuple-element.499), channel_id=1, source_target_pairs={{64,0},{68,4},{72,8},{76,12},{80,16},{84,20},{88,24},{92,28},{96,3... | collective-permute-start | bytes 786440 | tf_op jit(solution)/shard_map/ppermute | solution.py:15
  222.6 180.8 %collective-permute-start.24 = (bf16[128,1024]{1,0:T(8,128)(2,1)}, bf16[128,1024]{1,0:T(8,128)(2,1)}, u32[]{:S(2)}, u32[]{:S(2)}) collective-permute-start(bf16[128,1024]{1,0:T(8,128)(2,1)} %get-tuple-element.500), channel_id=1, source_target_pairs={{32,0},{36,4},{40,8},{44,12},{48,16},{52,20},{56,24},{60,28},{64,3... | collective-permute-start | bytes 786440 | tf_op jit(solution)/shard_map/ppermute | solution.py:15
  225.5 179.8 %collective-permute-start.23 = (bf16[128,1024]{1,0:T(8,128)(2,1)}, bf16[128,1024]{1,0:T(8,128)(2,1)}, u32[]{:S(2)}, u32[]{:S(2)}) collective-permute-start(bf16[128,1024]{1,0:T(8,128)(2,1)} %get-tuple-element.501), channel_id=1, source_target_pairs={{16,0},{20,4},{24,8},{28,12},{32,16},{36,20},{40,24},{44,28},{48,3... | collective-permute-start | bytes 786440 | tf_op jit(solution)/shard_map/ppermute | solution.py:15
  229.7 177.5 %collective-permute-start.22 = (bf16[128,1024]{1,0:T(8,128)(2,1)}, bf16[128,1024]{1,0:T(8,128)(2,1)}, u32[]{:S(2)}, u32[]{:S(2)}) collective-permute-start(bf16[128,1024]{1,0:T(8,128)(2,1)} %get-tuple-element.502), channel_id=1, source_target_pairs={{8,0},{12,4},{16,8},{20,12},{24,16},{28,20},{32,24},{36,28},{40,32... | collective-permute-start | bytes 786440 | tf_op jit(solution)/shard_map/ppermute | solution.py:15
  233.0 176.9 %collective-permute-start.14 = (bf16[128,1024]{1,0:T(8,128)(2,1)}, bf16[128,1024]{1,0:T(8,128)(2,1)}, u32[]{:S(2)}, u32[]{:S(2)}) collective-permute-start(bf16[128,1024]{1,0:T(8,128)(2,1)} %get-tuple-element.503), channel_id=1, source_target_pairs={{4,0},{8,4},{12,8},{16,12},{20,16},{24,20},{28,24},{32,28},{36,32}... | collective-permute-start | bytes 786440 | tf_op jit(solution)/shard_map/ppermute | solution.py:15
  235.8 179.5 %collective-permute-start.20 = (bf16[128,1024]{1,0:T(8,128)(2,1)}, bf16[128,1024]{1,0:T(8,128)(2,1)}, u32[]{:S(2)}, u32[]{:S(2)}) collective-permute-start(bf16[128,1024]{1,0:T(8,128)(2,1)} %get-tuple-element.504), channel_id=1, source_target_pairs={{256,0},{260,4},{264,8},{268,12},{272,16},{276,20},{280,24},{284,2... | collective-permute-start | bytes 786440 | tf_op jit(solution)/shard_map/ppermute | solution.py:15
  403.3 17.7 %collective-permute-start.19 = (bf16[128,1024]{1,0:T(8,128)(2,1)S(1)}, bf16[128,1024]{1,0:T(8,128)(2,1)S(1)}, u32[]{:S(2)}, u32[]{:S(2)}) collective-permute-start(bf16[128,1024]{1,0:T(8,128)(2,1)S(1)} %get-tuple-element.505), channel_id=1, source_target_pairs={{128,0},{132,4},{136,8},{140,12},{144,16},{148,20},{152,24},{156,2... | collective-permute-start | bytes 786440 | tf_op jit(solution)/shard_map/ppermute | solution.py:15
  405.3 15.8 %collective-permute-start.18 = (bf16[128,1024]{1,0:T(8,128)(2,1)S(1)}, bf16[128,1024]{1,0:T(8,128)(2,1)S(1)}, u32[]{:S(2)}, u32[]{:S(2)}) collective-permute-start(bf16[128,1024]{1,0:T(8,128)(2,1)S(1)} %get-tuple-element.506), channel_id=1, source_target_pairs={{64,0},{68,4},{72,8},{76,12},{80,16},{84,20},{88,24},{92,28},{96,3... | collective-permute-start | bytes 786440 | tf_op jit(solution)/shard_map/ppermute | solution.py:15
  410.0 29.4 %collective-permute-start.16 = (bf16[128,1024]{1,0:T(8,128)(2,1)S(1)}, bf16[128,1024]{1,0:T(8,128)(2,1)S(1)}, u32[]{:S(2)}, u32[]{:S(2)}) collective-permute-start(bf16[128,1024]{1,0:T(8,128)(2,1)S(1)} %get-tuple-element.508), channel_id=1, source_target_pairs={{16,0},{20,4},{24,8},{28,12},{32,16},{36,20},{40,24},{44,28},{48,3... | collective-permute-start | bytes 786440 | tf_op jit(solution)/shard_map/ppermute | solution.py:15
  415.3 30.2 %collective-permute-start.15 = (bf16[128,1024]{1,0:T(8,128)(2,1)S(1)}, bf16[128,1024]{1,0:T(8,128)(2,1)S(1)}, u32[]{:S(2)}, u32[]{:S(2)}) collective-permute-start(bf16[128,1024]{1,0:T(8,128)(2,1)S(1)} %get-tuple-element.509), channel_id=1, source_target_pairs={{8,0},{12,4},{16,8},{20,12},{24,16},{28,20},{32,24},{36,28},{40,32... | collective-permute-start | bytes 786440 | tf_op jit(solution)/shard_map/ppermute | solution.py:15
  (14 other events, 245.0 us)
